TPU v7x, 32 devices: a whole 2x2x4 slice. The times are simulated.
32 devices in a mesh: slab: 8 (over y, x, core), cross: 4 (over z).
Axes of the slice: x: 2, y: 2, z: 4, core: 2. Of those that a mesh axis runs over, the one named last changes fastest.
Arguments:
- source: float32 [8, 4, 4, 16, 256], P('slab', None, 'cross'), may hold values from -75 to 75
- reaction: float32 [8, 4, 4, 16, 256], P('slab', None, 'cross'), may hold values from 0.05 to 3
- counts: int32 [8], replicated, may hold values from 1 to 4, 16 in all
- orientation: int32 [8, 4, 4], P('slab', None, 'cross'), may hold values from 0 to 3
Outputs:
- potential: float32 [8, 4, 4, 16, 256], P('slab', None, 'cross')
- velocity: float32 [3, 8, 4, 4, 16, 256], P(None, 'slab', None, 'cross')
Inputs may be any that keep to these rules, and one draw needn't show every extreme that they name: counts sum to 16; the largest is 4.
All inputs are finite; a program needn't handle non-finite values.
Results may differ from a plain program's by a relative error of at most 0.0003.
Values sent between devices are 32-bit elements; how exact they have to be, the bound alone decides.
A program may use at most 64 MiB of HBM per device.

v0:
```python
import jax
import jax.numpy as jnp
import numpy as np
from jax import lax
from jax.sharding import PartitionSpec as P

ITERS = 2
LEVELS = 4
SWEEPS = 4


DAMPING = 0.8
LOCAL_SIDES = [[0, 1, 2, 3], [3, 2, 0, 1], [1, 0, 3, 2], [2, 3, 1, 0]]


def with_halo(block, sides, width):
    for axis, dim in sides:
        count = lax.axis_size(axis)
        forward = [(i, i + 1) for i in range(count - 1)]
        backward = [(target, source) for source, target in forward]
        low = lax.ppermute(
            lax.slice_in_dim(block, block.shape[dim] - width, None, axis=dim), axis, forward
        )
        high = lax.ppermute(lax.slice_in_dim(block, 0, width, axis=dim), axis, backward)
        block = jnp.concatenate([low, block, high], axis=dim)
    return block


def local_cell(turn_code, place_x, place_y, length):
    if turn_code == 0:
        return (place_x, place_y)
    if turn_code == 1:
        return (place_y, length - 1 - place_x)
    if turn_code == 2:
        return (length - 1 - place_x, length - 1 - place_y)
    return (length - 1 - place_y, place_x)


def face_table(length):
    table = np.zeros((4, 4, length * length), np.int32)
    offset = np.arange(length * length) // length
    depth = np.arange(length * length) % length
    for turn_code in range(4):
        for side_code in range(4):
            edge_value = 0 if side_code % 2 == 0 else length - 1
            fixed = offset * 0 + edge_value
            if side_code < 2:
                place_x, place_y = (fixed, offset)
            else:
                place_x, place_y = (offset, fixed)
            first, second = local_cell(turn_code, place_x, place_y, length)
            table[turn_code, side_code] = first * length * length + second * length + depth
    return table


def six_shifts(values, length):
    zero_rows = jnp.zeros_like(values[:, :1])
    next_u = jnp.concatenate([values[:, 1:], zero_rows], 1)
    prev_u = jnp.concatenate([zero_rows, values[:, :-1]], 1)
    zero_cols = jnp.zeros_like(values[..., :length])
    next_v = jnp.concatenate([values[..., length:], zero_cols], -1)
    prev_v = jnp.concatenate([zero_cols, values[..., :-length]], -1)
    depth = jnp.arange(length * length) % length
    zero_one = jnp.zeros_like(values[..., :1])
    next_w = jnp.where(depth != length - 1, jnp.concatenate([values[..., 1:], zero_one], -1), 0.0)
    prev_w = jnp.where(depth != 0, jnp.concatenate([zero_one, values[..., :-1]], -1), 0.0)
    return (next_u, prev_u, next_v, prev_v, next_w, prev_w)


def inner_neighbours(values, length):
    next_u, prev_u, next_v, prev_v, next_w, prev_w = six_shifts(values, length)
    return next_u + prev_u + next_v + prev_v + next_w + prev_w


def pair_matrix(length):
    half_size = length // 2
    rows_flat = jnp.arange(length * length)
    parent = rows_flat // length // 2 * half_size + rows_flat % length // 2
    return (parent[:, None] == jnp.arange(half_size * half_size)[None, :]).astype(jnp.float32)


def coarsen(values, length):
    half_size = length // 2
    slot_count = values.shape[0]
    summed = jnp.dot(
        values.reshape(-1, length * length), pair_matrix(length), precision=lax.Precision.HIGHEST
    )
    return summed.reshape(slot_count, half_size, 2, half_size * half_size).sum(2) * 0.125


def refine(values, length):
    half_size = length // 2
    slot_count = values.shape[0]
    spread = jnp.dot(
        values.reshape(-1, half_size * half_size),
        pair_matrix(length).T,
        precision=lax.Precision.HIGHEST,
    )
    return jnp.repeat(spread.reshape(slot_count, half_size, length * length), 2, axis=1)


def vcycle(forcing, coef_levels, size_levels, level_index):
    coef_level = coef_levels[level_index]
    length = size_levels[level_index]
    level_scale = 4.0 ** (-level_index)
    diagonal = 6.0 * level_scale + coef_level

    def level_apply(values):
        return (6.0 * values - inner_neighbours(values, length)) * level_scale + coef_level * values

    if level_index == LEVELS - 1:
        correction = jnp.zeros_like(forcing)
        for sweep_index in range(SWEEPS):
            correction = correction + DAMPING * (forcing - level_apply(correction)) / diagonal
        return correction
    correction = DAMPING * forcing / diagonal
    coarse = vcycle(
        coarsen(forcing - level_apply(correction), length),
        coef_levels,
        size_levels,
        level_index + 1,
    )
    correction = correction + refine(coarse, length)
    return correction + DAMPING * (forcing - level_apply(correction)) / diagonal


def take_cells(flat_values, indices):
    return flat_values[indices]


def local(source, reaction, counts, orientation):
    length = source.shape[3]
    slot_count = source.shape[1]
    cube_cells = length**3
    slab_place = lax.axis_index("slab")
    live_count = counts[slab_place]
    left_count = jnp.where(slab_place > 0, counts[jnp.maximum(slab_place - 1, 0)], 1)
    slot_ids = jnp.arange(slot_count)
    alive_mask = (slot_ids < live_count).astype(jnp.float32)[:, None, None]
    right_side = source[0, :, 0] * alive_mask
    coef_fine = reaction[0, :, 0]
    turn_codes = orientation[0, :, 0]
    face_index = jnp.asarray(face_table(length))[turn_codes]
    side_index = jnp.asarray(np.array(LOCAL_SIDES, np.int32))[turn_codes]
    coef_levels = [coef_fine]
    size_levels = [length]
    for level_index in range(LEVELS - 1):
        coef_levels.append(coarsen(coef_levels[-1], size_levels[-1]))
        size_levels.append(size_levels[-1] // 2)

    def place_ghosts(rims, indices, sides):
        empty = jnp.zeros((4, cube_cells), jnp.float32)
        return empty.at[jnp.broadcast_to(sides[:, None], indices.shape), indices].set(rims)

    def ghost_grid(values):
        face_cells = jax.vmap(take_cells)(values.reshape(slot_count, cube_cells), face_index)
        gathered = with_halo(face_cells[None, None], (("slab", 0), ("cross", 1)), 1)
        left_end = gathered[0, 1][left_count - 1, 1]
        right_start = gathered[2, 1][0, 0]
        lower_side = gathered[1, 0][:, 3]
        upper_side = gathered[1, 2][:, 2]
        later = jnp.concatenate([face_cells[1:, 0], jnp.zeros_like(face_cells[:1, 0])])
        plus_flow = jnp.where((slot_ids + 1 < live_count)[:, None], later, right_start[None])
        earlier = jnp.concatenate([jnp.zeros_like(face_cells[:1, 1]), face_cells[:-1, 1]])
        minus_flow = jnp.where((slot_ids == 0)[:, None], left_end[None], earlier)
        rims = jnp.stack([minus_flow, plus_flow, lower_side, upper_side], 1)
        placed = jax.vmap(place_ghosts)(rims, face_index, side_index)
        return placed.reshape(slot_count, 4, length, length * length)

    def precondition(values):
        return vcycle(values, coef_levels, size_levels, 0)

    def global_sum(first, second):
        return lax.psum(jnp.sum(first * second), ("slab", "cross"))

    solution = jnp.zeros_like(right_side)
    solution_rims = jnp.zeros((slot_count, 4, length, length * length), jnp.float32)
    residual = right_side
    smoothed = precondition(residual)
    direction = smoothed
    inner_now = global_sum(residual, smoothed)
    for iteration in range(ITERS):
        operate_ghosts = ghost_grid(direction)
        total = inner_neighbours(direction, length) + operate_ghosts.sum(1)
        image_vec = ((6.0 + coef_fine) * direction - total) * alive_mask
        step_size = inner_now / global_sum(direction, image_vec)
        solution = solution + step_size * direction
        solution_rims = solution_rims + step_size * operate_ghosts
        if iteration + 1 < ITERS:
            residual = residual - step_size * image_vec
            smoothed = precondition(residual)
            inner_next = global_sum(residual, smoothed)
            direction = smoothed + inner_next / inner_now * direction
            inner_now = inner_next
    ghosts = ghost_grid(solution)
    next_u, prev_u, next_v, prev_v, next_w, prev_w = six_shifts(solution, length)
    speed_u = 0.5 * (next_u + ghosts[:, 1] - (prev_u + ghosts[:, 0]))
    speed_v = 0.5 * (next_v + ghosts[:, 3] - (prev_v + ghosts[:, 2]))
    speed_w = 0.5 * (next_w - prev_w)
    velocity = jnp.stack([speed_u, speed_v, speed_w]) * alive_mask[None]
    return (solution[None, :, None], velocity[:, None, :, None])


def solution(mesh):
    in_specs = (
        P("slab", None, "cross", None, None),
        P("slab", None, "cross", None, None),
        P(),
        P("slab", None, "cross"),
    )
    out_specs = (P("slab", None, "cross", None, None), P(None, "slab", None, "cross", None, None))
    return jax.shard_map(local, mesh=mesh, in_specs=in_specs, out_specs=out_specs, check_vma=False)
```

profile of v0, /device:TPU:0, one launch (start us, length us, event | category | flops | bytes accessed | tf_op | source)
XLA Modules:
  0.0 345.8 jit_solution(3060932590081530972)
XLA Ops:
  0.6 1.3 fusion.315
  2.6 1.0 multiply_divide_fusion.1
  10.9 34.9 %gather_fusion.2 = f32[4096]{0:T(1024)S(1)} fusion(f32[4,4096]{1,0:T(4,128)S(1)} %bitcast.265, s32[4096]{0:T(1024)S(1)} %bitcast.268), kind=kCustom, calls=%fused_computation.2 | custom fusion | bytes 65536 | tf_op jit(solution)/shard_map/vmap()/gather | solution.py:128
  45.8 2.4 collective-permute-start
  48.2 1.3 collective-permute-start.1
  51.1 2.2 collective-permute-done.1
  53.4 3.5 %collective-permute-start.2 = (f32[3,1,4,4,256]{4,3,2,1,0:T(4,128)S(1)}, f32[3,1,4,4,256]{4,3,2,1,0:T(4,128)S(1)}, u32[]{:S(2)}, u32[]{:S(2)}) collective-permute-start(f32[3,1,4,4,256]{4,3,2,1,0:T(4,128)S(1)} %constant_dynamic-update-slice_fusion), channel_id=1, source_target_pairs={{0,1},{1,2},{2,3},{4,5},{5,6},{6,7},{8,9},{9,10},{10,11},{12,13},{... | collective-permute-start | bytes 147464 | tf_op jit(solution)/shard_map/ppermute | solution.py:21
  56.9 1.3 collective-permute-start.3
  58.6 4.2 %collective-permute-done.3 = f32[3,1,4,4,256]{4,3,2,1,0:T(4,128)S(1)} collective-permute-done((f32[3,1,4,4,256]{4,3,2,1,0:T(4,128)S(1)}, f32[3,1,4,4,256]{4,3,2,1,0:T(4,128)S(1)}, u32[]{:S(2)}, u32[]{:S(2)}) %collective-permute-start.3) | collective-permute-done | bytes 49184 | tf_op jit(solution)/shard_map/ppermute | solution.py:24
  62.9 15.6 %scatter_custom_fusion = f32[65536]{0:T(1024)S(1)} fusion(s32[4096]{0:T(1024)S(1)} %bitcast.302, f32[4096]{0:T(1024)S(1)} %bitcast.306, f32[]{:T(128)} %constant.392.clone.1), kind=kCustom, calls=%fused_computation.23 | custom fusion | bytes 262148
  78.8 0.7 multiply_reduce_fusion.1
  79.5 41.9 %all-reduce.132 = (f32[]{:T(128)}, f32[]{:T(128)}) all-reduce(f32[]{:T(128)} %get-tuple-element.7, f32[]{:T(128)} %get-tuple-element.6), channel_id=1, replica_groups=mesh['slab'=8,'cross'=4] {'slab','cross'}, use_global_device_ids=true, to_apply=%region_7.8 | all-reduce | flops 2 | bytes 16 | tf_op jit(solution)/shard_map/psum | solution.py:174
  126.2 0.7 multiply_reduce_fusion
  126.9 40.0 %psum.30 = f32[]{:T(128)} all-reduce(f32[]{:T(128)} %get-tuple-element.10), channel_id=1, replica_groups=mesh['slab'=8,'cross'=4] {'slab','cross'}, use_global_device_ids=true, to_apply=%region_16.17 | all-reduce | flops 1 | bytes 8 | tf_op jit(solution)/shard_map/psum | solution.py:174
  168.4 34.9 %gather_fusion.3 = f32[4096]{0:T(1024)S(1)} fusion(f32[4,4096]{1,0:T(4,128)S(1)} %bitcast.267, s32[4096]{0:T(1024)S(1)} %bitcast.269), kind=kCustom, calls=%fused_computation.3 | custom fusion | bytes 65536 | tf_op jit(solution)/shard_map/vmap()/gather | solution.py:128
  203.4 1.3 collective-permute-start.4
  204.7 1.3 collective-permute-start.5
  206.2 4.0 %collective-permute-done.5 = f32[1,1,4,4,256]{4,2,3,1,0:T(4,128)S(1)} collective-permute-done((f32[1,1,4,4,256]{4,2,3,1,0:T(4,128)S(1)}, f32[1,1,4,4,256]{4,2,3,1,0:T(4,128)S(1)}, u32[]{:S(2)}, u32[]{:S(2)}) %collective-permute-start.5) | collective-permute-done | bytes 16416 | tf_op jit(solution)/shard_map/ppermute | solution.py:24
  210.3 3.7 %collective-permute-start.6 = (f32[3,1,4,4,256]{4,2,3,1,0:T(4,128)S(1)}, f32[3,1,4,4,256]{4,2,3,1,0:T(4,128)S(1)}, u32[]{:S(2)}, u32[]{:S(2)}) collective-permute-start(f32[3,1,4,4,256]{4,2,3,1,0:T(4,128)S(1)} %constant_dynamic-update-slice_fusion.3), channel_id=1, source_target_pairs={{0,1},{1,2},{2,3},{4,5},{5,6},{6,7},{8,9},{9,10},{10,11},{12,13},{... | collective-permute-start | bytes 147464 | tf_op jit(solution)/shard_map/ppermute | solution.py:21
  213.9 1.3 collective-permute-start.7
  215.7 4.2 %collective-permute-done.7 = f32[3,1,4,4,256]{4,2,3,1,0:T(4,128)S(1)} collective-permute-done((f32[3,1,4,4,256]{4,2,3,1,0:T(4,128)S(1)}, f32[3,1,4,4,256]{4,2,3,1,0:T(4,128)S(1)}, u32[]{:S(2)}, u32[]{:S(2)}) %collective-permute-start.7) | collective-permute-done | bytes 49184 | tf_op jit(solution)/shard_map/ppermute | solution.py:24
  220.0 15.6 %scatter_custom_fusion.1 = f32[65536]{0:T(1024)S(1)} fusion(s32[4096]{0:T(1024)S(1)} %bitcast.303, f32[4096]{0:T(1024)S(1)} %bitcast.307, f32[]{:T(128)} %constant.392.clone.1), kind=kCustom, calls=%fused_computation.21 | custom fusion | bytes 262148
  236.6 40.9 %psum.31 = f32[]{:T(128)} all-reduce(f32[]{:T(128)} %fusion.10), channel_id=1, replica_groups=mesh['slab'=8,'cross'=4] {'slab','cross'}, use_global_device_ids=true, to_apply=%region_20.21 | all-reduce | flops 1 | bytes 8 | tf_op jit(solution)/shard_map/psum | solution.py:174
  278.9 34.9 %gather_fusion.4 = f32[4096]{0:T(1024)S(1)} fusion(f32[4,4096]{1,0:T(4,128)S(1)} %bitcast.266, s32[4096]{0:T(1024)S(1)} %bitcast.270), kind=kCustom, calls=%fused_computation.4 | custom fusion | bytes 65536 | tf_op jit(solution)/shard_map/vmap()/gather | solution.py:128
  313.9 1.3 collective-permute-start.8
  315.2 1.3 collective-permute-start.9
  316.9 3.9 %collective-permute-done.9 = f32[1,1,4,4,256]{4,2,3,1,0:T(4,128)S(1)} collective-permute-done((f32[1,1,4,4,256]{4,2,3,1,0:T(4,128)S(1)}, f32[1,1,4,4,256]{4,2,3,1,0:T(4,128)S(1)}, u32[]{:S(2)}, u32[]{:S(2)}) %collective-permute-start.9) | collective-permute-done | bytes 16416 | tf_op jit(solution)/shard_map/ppermute | solution.py:24
  320.8 2.5 collective-permute-start.10
  323.3 1.3 collective-permute-start.11
  325.0 4.2 %collective-permute-done.11 = f32[3,1,4,4,256]{4,2,3,1,0:T(4,128)S(1)} collective-permute-done((f32[3,1,4,4,256]{4,2,3,1,0:T(4,128)S(1)}, f32[3,1,4,4,256]{4,2,3,1,0:T(4,128)S(1)}, u32[]{:S(2)}, u32[]{:S(2)}) %collective-permute-start.11) | collective-permute-done | bytes 49184 | tf_op jit(solution)/shard_map/ppermute | solution.py:24
  329.3 15.6 %scatter_custom_fusion.2 = f32[65536]{0:T(1024)S(1)} fusion(s32[4096]{0:T(1024)S(1)} %bitcast.304, f32[4096]{0:T(1024)S(1)} %bitcast.305, f32[]{:T(128)} %constant.392.clone.1), kind=kCustom, calls=%fused_computation.19 | custom fusion | bytes 262148
  345.1 0.8 fusion
  (233 shorter events, 15.3 us)
Async XLA Ops:
  3.6 0.8 copy-start
  3.6 0.9 copy-start.2
  8.2 0.7 copy-start.7
  8.2 0.7 copy-start.3
  9.5 0.7 copy-start.4
  45.8 5.3 %collective-permute-start = (f32[1,1,4,4,256]{4,3,2,1,0:T(4,128)S(1)}, f32[1,1,4,4,256]{4,3,2,1,0:T(4,128)S(1)}, u32[]{:S(2)}, u32[]{:S(2)}) collective-permute-start(f32[1,1,4,4,256]{4,3,2,1,0:T(4,128)S(1)} %broadcast_in_dim.388), channel_id=1, source_target_pairs={{0,4},{4,8},{8,12},{12,16},{16,20},{20,24},{24,28},{1,5},{5,9},{9,... | collective-permute-start | bytes 49160 | tf_op jit(solution)/shard_map/ppermute | solution.py:21
  48.2 5.2 %collective-permute-start.1 = (f32[1,1,4,4,256]{4,3,2,1,0:T(4,128)S(1)}, f32[1,1,4,4,256]{4,3,2,1,0:T(4,128)S(1)}, u32[]{:S(2)}, u32[]{:S(2)}) collective-permute-start(f32[1,1,4,4,256]{4,3,2,1,0:T(4,128)S(1)} %broadcast_in_dim.388), channel_id=1, source_target_pairs={{4,0},{8,4},{12,8},{16,12},{20,16},{24,20},{28,24},{5,1},{9,5},{13... | collective-permute-start | bytes 49160 | tf_op jit(solution)/shard_map/ppermute | solution.py:24
  49.5 0.7 copy-start.6
  49.5 0.7 copy-start.5
  53.4 5.2 %collective-permute-start.2 = (f32[3,1,4,4,256]{4,3,2,1,0:T(4,128)S(1)}, f32[3,1,4,4,256]{4,3,2,1,0:T(4,128)S(1)}, u32[]{:S(2)}, u32[]{:S(2)}) collective-permute-start(f32[3,1,4,4,256]{4,3,2,1,0:T(4,128)S(1)} %constant_dynamic-update-slice_fusion), channel_id=1, source_target_pairs={{0,1},{1,2},{2,3},{4,5},{5,6},{6,7},{8,9},{9,10},{10,11},{12,13},{... | collective-permute-start | bytes 147464 | tf_op jit(solution)/shard_map/ppermute | solution.py:21
  56.9 6.0 %collective-permute-start.3 = (f32[3,1,4,4,256]{4,3,2,1,0:T(4,128)S(1)}, f32[3,1,4,4,256]{4,3,2,1,0:T(4,128)S(1)}, u32[]{:S(2)}, u32[]{:S(2)}) collective-permute-start(f32[3,1,4,4,256]{4,3,2,1,0:T(4,128)S(1)} %constant_dynamic-update-slice_fusion), channel_id=1, source_target_pairs={{1,0},{2,1},{3,2},{5,4},{6,5},{7,6},{9,8},{10,9},{11,10},{13,12},{... | collective-permute-start | bytes 147464 | tf_op jit(solution)/shard_map/ppermute | solution.py:24
  203.4 2.8 collective-permute-start.4
  204.7 5.6 %collective-permute-start.5 = (f32[1,1,4,4,256]{4,2,3,1,0:T(4,128)S(1)}, f32[1,1,4,4,256]{4,2,3,1,0:T(4,128)S(1)}, u32[]{:S(2)}, u32[]{:S(2)}) collective-permute-start(f32[1,1,4,4,256]{4,2,3,1,0:T(4,128)S(1)} %copy.65), channel_id=1, source_target_pairs={{4,0},{8,4},{12,8},{16,12},{20,16},{24,20},{28,24},{5,1},{9,5},{13... | collective-permute-start | bytes 49160 | tf_op jit(solution)/shard_map/ppermute | solution.py:24
  210.3 5.4 %collective-permute-start.6 = (f32[3,1,4,4,256]{4,2,3,1,0:T(4,128)S(1)}, f32[3,1,4,4,256]{4,2,3,1,0:T(4,128)S(1)}, u32[]{:S(2)}, u32[]{:S(2)}) collective-permute-start(f32[3,1,4,4,256]{4,2,3,1,0:T(4,128)S(1)} %constant_dynamic-update-slice_fusion.3), channel_id=1, source_target_pairs={{0,1},{1,2},{2,3},{4,5},{5,6},{6,7},{8,9},{9,10},{10,11},{12,13},{... | collective-permute-start | bytes 147464 | tf_op jit(solution)/shard_map/ppermute | solution.py:21
  213.9 6.0 %collective-permute-start.7 = (f32[3,1,4,4,256]{4,2,3,1,0:T(4,128)S(1)}, f32[3,1,4,4,256]{4,2,3,1,0:T(4,128)S(1)}, u32[]{:S(2)}, u32[]{:S(2)}) collective-permute-start(f32[3,1,4,4,256]{4,2,3,1,0:T(4,128)S(1)} %constant_dynamic-update-slice_fusion.3), channel_id=1, source_target_pairs={{1,0},{2,1},{3,2},{5,4},{6,5},{7,6},{9,8},{10,9},{11,10},{13,12},{... | collective-permute-start | bytes 147464 | tf_op jit(solution)/shard_map/ppermute | solution.py:24
  278.8 37.7 %copy-start.1 = (f32[4,16,256]{2,1,0:T(8,128)}, f32[4,16,256]{2,1,0:T(8,128)S(1)}, u32[]{:S(2)}) copy-start(f32[4,16,256]{2,1,0:T(8,128)S(1)} %multiply_add_fusion) | copy-start | bytes 196612
  313.9 2.9 collective-permute-start.8
  315.2 5.6 %collective-permute-start.9 = (f32[1,1,4,4,256]{4,2,3,1,0:T(4,128)S(1)}, f32[1,1,4,4,256]{4,2,3,1,0:T(4,128)S(1)}, u32[]{:S(2)}, u32[]{:S(2)}) collective-permute-start(f32[1,1,4,4,256]{4,2,3,1,0:T(4,128)S(1)} %copy.71), channel_id=1, source_target_pairs={{4,0},{8,4},{12,8},{16,12},{20,16},{24,20},{28,24},{5,1},{9,5},{13... | collective-permute-start | bytes 49160 | tf_op jit(solution)/shard_map/ppermute | solution.py:24
  320.8 4.2 %collective-permute-start.10 = (f32[3,1,4,4,256]{4,2,3,1,0:T(4,128)S(1)}, f32[3,1,4,4,256]{4,2,3,1,0:T(4,128)S(1)}, u32[]{:S(2)}, u32[]{:S(2)}) collective-permute-start(f32[3,1,4,4,256]{4,2,3,1,0:T(4,128)S(1)} %constant_dynamic-update-slice_fusion.6), channel_id=1, source_target_pairs={{0,1},{1,2},{2,3},{4,5},{5,6},{6,7},{8,9},{9,10},{10,11},{12,13},{... | collective-permute-start | bytes 147464 | tf_op jit(solution)/shard_map/ppermute | solution.py:21
  323.3 6.0 %collective-permute-start.11 = (f32[3,1,4,4,256]{4,2,3,1,0:T(4,128)S(1)}, f32[3,1,4,4,256]{4,2,3,1,0:T(4,128)S(1)}, u32[]{:S(2)}, u32[]{:S(2)}) collective-permute-start(f32[3,1,4,4,256]{4,2,3,1,0:T(4,128)S(1)} %constant_dynamic-update-slice_fusion.6), channel_id=1, source_target_pairs={{1,0},{2,1},{3,2},{5,4},{6,5},{7,6},{9,8},{10,9},{11,10},{13,12},{... | collective-permute-start | bytes 147464 | tf_op jit(solution)/shard_map/ppermute | solution.py:24
where the time goes:
time: 348 us; the launch traced here: 346 us
  local copies, waits for them, and re-layouts  161 us (46%)
  blocking collectives  123 us (35%)
  waiting for transfers between devices  23.7 us (7%)
  starting transfers between devices  22.3 us (6%)
  other arithmetic  7.4 us (2%)
  between operations  6.41 us (2%)
    psum x3, blocking collectives, global_sum(): return lax.psum(jnp.sum(first * second), ('slab', 'cross'))  123 us
    gather x6, local copies, waits for them, and re-layouts, take_cells(): return flat_values[indices]  105 us
    unnamed x40, local copies, waits for them, and re-layouts  49.2 us
    ppermute x6, waiting for transfers between devices, with_halo(): lax.ppermute(lax.slice_in_dim(block, 0, width, axis=dim), axis, backward)  22.9 us
    ppermute x6, starting transfers between devices, with_halo(): lax.ppermute(lax.slice_in_dim(block, block.shape[dim] - width, None, axis...  14.6 us
    ppermute x6, starting transfers between devices, with_halo(): lax.ppermute(lax.slice_in_dim(block, 0, width, axis=dim), axis, backward)  7.75 us
  transfers between devices with their start and end apart: 12, of which 9 were waited for; matrix products, arithmetic and copies ran while one was open for 0% of the time, Pallas kernels for 0%

commit v1 on v0

v1 whole, which is shorter than its diff:
```python
import functools

import jax
import jax.numpy as jnp
from jax import lax
from jax.experimental import pallas as pl
from jax.experimental.pallas import tpu as pltpu
from jax.sharding import PartitionSpec as P

LEVELS = 4
SWEEPS = 4
DAMPING = 0.8
KEEP = 1.0 - DAMPING


def roll(x, shift, axis):
    return pltpu.roll(x, shift % x.shape[axis], axis)


def iota(shape, axis):
    return lax.broadcasted_iota(jnp.int32, shape, axis)


def keep(mask, x):
    return jnp.where(mask, x, 0.0)


class Grid:
    def __init__(self):
        self.u = iota((128, 128), 0) % 16
        self.w = iota((128, 128), 1) % 16
        self.g = iota((64, 128), 1) // 16
        self.gg = iota((128, 128), 1) // 16

    def shifts(self, x, d):
        prev_u = keep(self.u >= d, roll(x, d, 0))
        next_u = keep(self.u < 16 - d, roll(x, -d, 0))
        prev_w = keep(self.w >= d, roll(x, d, 1))
        next_w = keep(self.w < 16 - d, roll(x, -d, 1))
        up = roll(x, 16 * d, 1)
        down = roll(x, -16 * d, 1)
        inside = self.g >= d
        prev_v = jnp.concatenate([keep(inside, up[:64]), jnp.where(inside, up[64:], up[:64])], 0)
        inside = self.g < 8 - d
        next_v = jnp.concatenate([jnp.where(inside, down[:64], down[64:]), keep(inside, down[64:])], 0)
        return prev_u, next_u, prev_v, next_v, prev_w, next_w

    def near(self, x, d):
        if d == 8:
            swap_u = x.reshape(8, 2, 8, 128)
            swap_u = jnp.concatenate([swap_u[:, 1:], swap_u[:, :1]], 1).reshape(128, 128)
            swap_v = jnp.concatenate([x[64:], x[:64]], 0)
            swap_w = jnp.where(self.w >= 8, roll(x, 8, 1), roll(x, -8, 1))
            return swap_u + swap_v + swap_w
        prev_u, next_u, prev_v, next_v, prev_w, next_w = self.shifts(x, d)
        return (prev_u + next_u) + (prev_v + next_v) + (prev_w + next_w)

    def restrict(self, x, d):
        x = x + jnp.where((self.u & d) != 0, roll(x, d, 0), roll(x, -d, 0))
        if d == 4:
            x = x + roll(x, 64, 1)
        else:
            x = x + jnp.where((self.gg & d) != 0, roll(x, 16 * d, 1), roll(x, -16 * d, 1))
        x = x + jnp.where((self.w & d) != 0, roll(x, d, 1), roll(x, -d, 1))
        return x * 0.125


def vcycle(grid, f, inverse, level):
    d = 2**level
    scale = 4.0**-level
    inv = inverse[level]
    e = inv * f
    if level == LEVELS - 1:
        for _ in range(SWEEPS - 1):
            e = KEEP * e + inv * (f + scale * grid.near(e, d))
        return e
    e = e + vcycle(grid, grid.restrict(KEEP * f + scale * grid.near(e, d), d), inverse, level + 1)
    return KEEP * e + inv * (f + scale * grid.near(e, d))


def fold(x):
    return x.reshape(8, 8, 128).sum(1)


def unfold(x):
    return jnp.broadcast_to(x[:, None, :], (8, 8, 128)).reshape(64, 128)


def spread(x):
    x = x + roll(x, 16, 1)
    x = x + roll(x, 32, 1)
    return x + roll(x, 64, 1)


def flip(x):
    row = iota(x.shape, 0)
    group = iota(x.shape, 1) // 16
    x = jnp.where(row % 2 == 1, roll(x, 1, 0), roll(x, -1, 0))
    x = roll(x, 64, 1)
    x = jnp.where((group & 2) != 0, roll(x, 32, 1), roll(x, -32, 1))
    return jnp.where((group & 1) != 0, roll(x, 16, 1), roll(x, -16, 1))


def pick(turn, a, b, c, d):
    return jnp.where(turn == 0, a, jnp.where(turn == 1, b, jnp.where(turn == 2, c, d)))


def kernel(
    n_slab, n_cross, counts_ref, turn_ref, source_ref, reaction_ref, pot_ref, vel_ref,
    out_face, in_face, face_send, face_recv, mine, sums, sum_send, sum_recv,
    mine_z, sums_z, sum_send_z, sum_recv_z,
):
    slab = lax.axis_index("slab")
    cross = lax.axis_index("cross")

    in_face[...] = jnp.zeros_like(in_face)
    barrier = pltpu.get_barrier_semaphore()

    def each(count, body):
        if count <= 8:
            for step in range(1, count):
                body(step)
        else:
            lax.fori_loop(1, count, lambda step, carry: (body(step), carry)[1], 0)

    def greet_slab(step):
        pl.semaphore_signal(barrier, inc=1, device_id=(lax.rem(slab + step, n_slab), cross), device_id_type=pl.DeviceIdType.MESH)

    def greet_cross(step):
        pl.semaphore_signal(barrier, inc=1, device_id=(slab, lax.rem(cross + step, n_cross)), device_id_type=pl.DeviceIdType.MESH)

    each(n_slab, greet_slab)
    each(n_cross, greet_cross)

    grid = Grid()
    live = counts_ref[slab]
    row8 = iota((8, 128), 0)
    turn = jnp.where(row8 < 2, turn_ref[0], jnp.where(row8 < 4, turn_ref[1], jnp.where(row8 < 6, turn_ref[2], turn_ref[3])))
    alive = (iota((128, 128), 0) % 64) // 16 < live
    u64 = grid.u[:64]
    diagonal_face = u64 % 8 == grid.g

    def load(ref):
        x = ref[...]
        return jnp.concatenate([x[:, :128], x[:, 128:]], 0)

    r0 = keep(alive, load(source_ref))
    coef = jnp.where(alive, load(reaction_ref), 1.0)
    inverse = []
    level_coef = coef
    for level in range(LEVELS):
        inverse.append(DAMPING / (6.0 * 4.0**-level + level_coef))
        if level + 1 < LEVELS:
            level_coef = grid.restrict(level_coef, 2**level)

    def faces(x):
        lo, hi = x[:64], x[64:]
        u0 = fold(keep(u64 == 0, lo)) + roll(fold(keep(u64 == 0, hi)), 1, 0)
        u1 = roll(fold(keep(u64 == 15, lo)), -1, 0) + fold(keep(u64 == 15, hi))
        v0 = fold(keep(diagonal_face, spread(keep(grid.g == 0, lo))))
        v1 = fold(keep(diagonal_face, spread(keep(grid.g == 7, hi))))
        flipped = flip(jnp.concatenate([u0, u1, v0, v1], 0))
        fu0, fu1, fv0, fv1 = flipped[:8], flipped[8:16], flipped[16:24], flipped[24:]
        return (
            pick(turn, u0, v1, fu1, fv0),
            pick(turn, u1, v0, fu0, fv1),
            pick(turn, v0, fu0, fv1, u1),
            pick(turn, v1, fu1, fv0, u0),
        )

    sides = (
        (slab + 1 < n_slab, slab > 0, (slab + 1, cross)),
        (slab > 0, slab + 1 < n_slab, (slab - 1, cross)),
        (cross + 1 < n_cross, cross > 0, (slab, cross + 1)),
        (cross > 0, cross + 1 < n_cross, (slab, cross - 1)),
    )

    def face_copy(turn_of, side):
        return pltpu.make_async_remote_copy(
            src_ref=out_face.at[turn_of, side],
            dst_ref=in_face.at[turn_of, side],
            send_sem=face_send.at[turn_of, side],
            recv_sem=face_recv.at[turn_of, side],
            device_id=sides[side][2],
            device_id_type=pl.DeviceIdType.MESH,
        )

    def exchange_start(turn_of, x):
        x0, x1, y0, y1 = faces(x)
        last = jnp.where(live == 1, x1, jnp.where(live == 2, roll(x1, -2, 0), jnp.where(live == 3, roll(x1, -4, 0), roll(x1, -6, 0))))
        out_face[turn_of, 0] = last
        out_face[turn_of, 1] = x0
        out_face[turn_of, 2] = y1
        out_face[turn_of, 3] = y0
        for side in range(4):
            @pl.when(sides[side][0])
            def _():
                face_copy(turn_of, side).start()
        return x0, x1

    def exchange_end(turn_of, x0, x1):
        for side in range(4):
            @pl.when(sides[side][1])
            def _():
                face_copy(turn_of, side).wait_recv()
        right = keep(row8 < 2, in_face[turn_of, 1])
        right = right + roll(right, 2, 0)
        right = right + roll(right, 4, 0)
        gx0 = jnp.where(row8 < 2, in_face[turn_of, 0], roll(x1, 2, 0))
        gx1 = jnp.where(row8 < 2 * (live - 1), roll(x0, -2, 0), right)
        gy0 = in_face[turn_of, 2]
        gy1 = in_face[turn_of, 3]
        flipped = flip(jnp.concatenate([gx0, gx1, gy0, gy1], 0))
        fx0, fx1, fy0, fy1 = flipped[:8], flipped[8:16], flipped[16:24], flipped[24:]
        gu0 = pick(turn, gx0, fy0, fx1, gy1)
        gu1 = pick(turn, gx1, fy1, fx0, gy0)
        gv0 = pick(turn, gy0, gx1, fy1, fx0)
        gv1 = pick(turn, gy1, gx0, fy0, fx1)
        lo = jnp.where(u64 == 0, unfold(gu0), keep(u64 == 15, unfold(roll(gu1, 1, 0))))
        hi = jnp.where(u64 == 0, unfold(roll(gu0, -1, 0)), keep(u64 == 15, unfold(gu1)))
        rim_u = jnp.concatenate([lo, hi], 0)
        lo = keep(grid.g == 0, spread(keep(diagonal_face, unfold(gv0))))
        hi = keep(grid.g == 7, spread(keep(diagonal_face, unfold(gv1))))
        rim_v = jnp.concatenate([lo, hi], 0)
        return rim_u, rim_v

    def operate(x, rim_u, rim_v):
        return keep(alive, (6.0 + coef) * x - (grid.near(x, 1) + (rim_u + rim_v)))

    def inner(a, b):
        return (a * b).reshape(16, 8, 128).sum(0)

    z0 = vcycle(grid, r0, inverse, 0)
    pl.semaphore_wait(barrier, n_slab - 1 + n_cross - 1)
    z_faces = exchange_start(0, z0)
    dot_rz = inner(r0, z0)
    z_rims = exchange_end(0, *z_faces)
    q0 = operate(z0, *z_rims)
    w0 = vcycle(grid, q0, inverse, 0)
    w_faces = exchange_start(1, w0)
    dot_zq = inner(z0, q0)
    dot_rw = inner(r0, w0)
    dot_qw = inner(q0, w0)
    w_rims = exchange_end(1, *w_faces)
    dot_wv = inner(w0, operate(w0, *w_rims))
    none = jnp.zeros((8, 128), jnp.float32)
    partial = jnp.concatenate([dot_rz, dot_zq, dot_rw, dot_qw, dot_wv, none, none, none], 0)
    partial = partial.reshape(8, 8, 128).sum(1)

    def total(value, own, count, me, out, into, send, recv, place):
        out[...] = value

        def copy(source, target):
            return pltpu.make_async_remote_copy(
                src_ref=out, dst_ref=into.at[source], send_sem=send.at[target], recv_sem=recv.at[source],
                device_id=place(target), device_id_type=pl.DeviceIdType.MESH,
            )

        def begin(step):
            copy(me, lax.rem(me + step, count)).start()

        def arrive(step):
            copy(lax.rem(me + step, count), lax.rem(me + step, count)).wait_recv()

        def leave(step):
            copy(me, lax.rem(me + step, count)).wait_send()

        each(count, begin)
        into[me] = value
        each(count, arrive)
        result = into[...].sum(0)
        return result, lambda: each(count, leave)

    across, leave_slab = total(partial, slab, n_slab, slab, mine, sums, sum_send, sum_recv, lambda k: (k, cross))
    whole, leave_cross = total(across, cross, n_cross, cross, mine_z, sums_z, sum_send_z, sum_recv_z, lambda k: (slab, k))
    whole = jnp.sum(whole, 1, keepdims=True)
    rz, zq, rw, qw, wv = (whole[k : k + 1] for k in range(5))
    alpha = rz / zq
    rz_new = rz - alpha * (zq + rw) + alpha * alpha * qw
    gain = 1.0 + rz_new / rz
    pq = gain * gain * zq - 2.0 * gain * alpha * qw + alpha * alpha * wv
    step = rz_new / pq
    of_z = alpha + step * gain
    of_w = -step * alpha
    x = of_z * z0 + of_w * w0
    rim_u = of_z * z_rims[0] + of_w * w_rims[0]
    rim_v = of_z * z_rims[1] + of_w * w_rims[1]
    prev_u, next_u, prev_v, next_v, prev_w, next_w = grid.shifts(x, 1)
    rim_u = jnp.where(grid.u == 0, -rim_u, rim_u)
    rim_v = jnp.concatenate([-rim_v[:64], rim_v[64:]], 0)

    def store(ref, value):
        ref[...] = jnp.concatenate([value[:64], value[64:]], 1)

    store(pot_ref, x)
    store(vel_ref.at[0], keep(alive, 0.5 * (next_u - prev_u + rim_u)))
    store(vel_ref.at[1], keep(alive, 0.5 * (next_v - prev_v + rim_v)))
    store(vel_ref.at[2], keep(alive, 0.5 * (next_w - prev_w)))

    leave_slab()
    leave_cross()
    for turn_of in range(2):
        for side in range(4):
            @pl.when(sides[side][0])
            def _():
                face_copy(turn_of, side).wait_send()


def local(n_slab, n_cross, source, reaction, counts, orientation):
    slots, length = source.shape[1], source.shape[3]
    rows, lanes = slots * length, length * length
    dma = pltpu.SemaphoreType.DMA
    vmem = pl.BlockSpec(memory_space=pltpu.VMEM)
    smem = pl.BlockSpec(memory_space=pltpu.SMEM)
    potential, velocity = pl.pallas_call(
        functools.partial(kernel, n_slab, n_cross),
        out_shape=(
            jax.ShapeDtypeStruct((rows, lanes), jnp.float32),
            jax.ShapeDtypeStruct((3, rows, lanes), jnp.float32),
        ),
        in_specs=[smem, smem, vmem, vmem],
        out_specs=(vmem, vmem),
        scratch_shapes=[
            pltpu.VMEM((2, 4, 8, 128), jnp.float32),
            pltpu.VMEM((2, 4, 8, 128), jnp.float32),
            dma((2, 4)),
            dma((2, 4)),
            pltpu.VMEM((8, 128), jnp.float32),
            pltpu.VMEM((n_slab, 8, 128), jnp.float32),
            dma((n_slab,)),
            dma((n_slab,)),
            pltpu.VMEM((8, 128), jnp.float32),
            pltpu.VMEM((n_cross, 8, 128), jnp.float32),
            dma((n_cross,)),
            dma((n_cross,)),
        ],
        compiler_params=pltpu.CompilerParams(
            collective_id=0, has_side_effects=True, vmem_limit_bytes=16 * 2**20
        ),
    )(counts, orientation.reshape(slots), source.reshape(rows, lanes), reaction.reshape(rows, lanes))
    return potential.reshape(source.shape), velocity.reshape((3,) + source.shape)


def solution(mesh):
    spec = P("slab", None, "cross", None, None)
    return jax.shard_map(
        functools.partial(local, mesh.shape["slab"], mesh.shape["cross"]),
        mesh=mesh,
        in_specs=(spec, spec, P(), P("slab", None, "cross")),
        out_specs=(spec, P(None, "slab", None, "cross", None, None)),
        check_vma=False,
    )
```

time: 348 us -> 26.8 us (0.08)
  local copies, waits for them, and re-layouts: 161 us -> 3.64 us
  blocking collectives: 123 us -> 0 us
  waiting for transfers between devices: 23.7 us -> 0 us
  Pallas kernels: 0 us -> 22.3 us
  starting transfers between devices: 22.3 us -> 0 us
  other arithmetic: 7.4 us -> 0 us
  between operations: 6.41 us -> 0.66 us
    psum x3 -> x0, blocking collectives: 123 us -> none  [global_sum(): return lax.psum(jnp.sum(first * second), ('slab', 'cross'))]
    gather x8 -> x0, local copies, waits for them, and re-layouts: 106 us -> none  [the longest x6 105 us: take_cells(): return flat_values[indices]]
    unnamed x40 -> x10, local copies, waits for them, and re-layouts: 49.2 us -> 3.64 us
    ppermute x12 -> x0, waiting for transfers between devices: 23.7 us -> none  [the longest x6 22.9 us: with_halo(): lax.ppermute(lax.slice_in_dim(block, 0, width, axis=dim), axis, backward)]
    ppermute x12 -> x0, starting transfers between devices: 22.3 us -> none  [the longest x6 14.6 us: with_halo(): lax.ppermute(lax.slice_in_dim(block, block.shape[dim] - width, None, axis...]
    pallas_call x0 -> x1, Pallas kernels: none -> 22.3 us  [local(): pl.pallas_call(functools.partial(kernel, n_slab, n_cross), out_shape=(jax...]
  transfers between devices with their start and end apart: 12 -> 0, of which waited for: 9 -> 0; matrix products, arithmetic and copies ran while one was open for 0% -> 0% of each run, Pallas kernels for 0% -> 0%
where the time goes in v1:
time: 26.8 us; the launch traced here: 26.6 us
  Pallas kernels  22.3 us (83%)
  local copies, waits for them, and re-layouts  3.64 us (14%)
  between operations  0.66 us (2%)
    pallas_call x1, Pallas kernels, local(): pl.pallas_call(functools.partial(kernel, n_slab, n_cross), out_shape=(jax...  22.3 us
    unnamed x10, local copies, waits for them, and re-layouts  3.64 us

profile of v1, /device:TPU:0, one launch (start us, length us, event | category | flops | bytes accessed | tf_op | source)
XLA Modules:
  0.0 26.6 jit_solution(5419718602975843852)
XLA Ops:
  0.6 0.0 copy-start.2
  0.6 0.0 copy-start.3
  0.7 0.6 %copy-done.2 = s32[8]{0:T(128)S(1)} copy-done((s32[8]{0:T(128)S(1)}, s32[8]{0:T(128)}, u32[]{:S(2)}) %copy-start.2) | copy-done | bytes 56
  1.3 0.0 copy-done.3
  1.3 0.0 copy-start
  1.3 0.8 %copy-done = f32[1,4,1,16,256]{4,3,2,1,0:T(8,128)S(1)} copy-done((f32[1,4,1,16,256]{4,3,2,1,0:T(8,128)S(1)}, f32[1,4,1,16,256]{4,3,2,1,0:T(8,128)}, u32[]{:S(2)}) %copy-start) | copy-done | bytes 65560
  2.1 0.0 copy-start.1
  2.1 0.8 %copy-done.1 = f32[1,4,1,16,256]{4,3,2,1,0:T(8,128)S(1)} copy-done((f32[1,4,1,16,256]{4,3,2,1,0:T(8,128)S(1)}, f32[1,4,1,16,256]{4,3,2,1,0:T(8,128)}, u32[]{:S(2)}) %copy-start.1) | copy-done | bytes 65560
  3.0 22.3 %shard_map.59 = (f32[64,256]{1,0:T(8,128)S(1)}, f32[3,64,256]{2,1,0:T(8,128)S(1)}) custom-call(s32[8]{0:T(128)S(1)} %copy-done.2, s32[4]{0:T(128)S(1)} %bitcast.13, f32[64,256]{1,0:T(8,128)S(1)} %bitcast.10, f32[64,256]{1,0:T(8,128)S(1)} %bitcast.11), custom_call_target="tpu_custom_call" | custom-call | tf_op jit(solution)/shard_map/pallas_call | solution.py:315
  25.3 0.6 %copy.10 = f32[1,4,1,16,256]{4,3,2,1,0:T(8,128)} copy(f32[1,4,1,16,256]{4,3,2,1,0:T(8,128)S(1)} %bitcast.12) | data formatting | bytes 131072
  25.9 0.7 %copy.11 = f32[3,1,4,1,16,256]{5,4,3,2,1,0:T(8,128)} copy(f32[3,1,4,1,16,256]{5,4,3,2,1,0:T(8,128)S(1)} %bitcast.9) | data formatting | bytes 393216
Async XLA Ops:
  0.6 0.7 %copy-start.2 = (s32[8]{0:T(128)S(1)}, s32[8]{0:T(128)}, u32[]{:S(2)}) copy-start(s32[8]{0:T(128)} %counts_ref.1) | copy-start | bytes 100
  0.6 0.7 %copy-start.3 = (s32[1,4,1]{1,2,0:T(1,128)S(1)}, s32[1,4,1]{1,2,0:T(1,128)}, u32[]{:S(2)}) copy-start(s32[1,4,1]{1,2,0:T(1,128)} %param.7) | copy-start | bytes 52
  1.3 0.8 %copy-start = (f32[1,4,1,16,256]{4,3,2,1,0:T(8,128)S(1)}, f32[1,4,1,16,256]{4,3,2,1,0:T(8,128)}, u32[]{:S(2)}) copy-start(f32[1,4,1,16,256]{4,3,2,1,0:T(8,128)} %param.4) | copy-start | bytes 196612
  2.1 0.8 %copy-start.1 = (f32[1,4,1,16,256]{4,3,2,1,0:T(8,128)S(1)}, f32[1,4,1,16,256]{4,3,2,1,0:T(8,128)}, u32[]{:S(2)}) copy-start(f32[1,4,1,16,256]{4,3,2,1,0:T(8,128)} %param.5) | copy-start | bytes 196612

commit v2 on v1

--- a/solution.py
+++ b/solution.py
@@ -106,12 +106,19 @@
 
 
 def kernel(
-    n_slab, n_cross, counts_ref, turn_ref, source_ref, reaction_ref, pot_ref, vel_ref,
+    n_slab, n_cross, counts_hbm, turn_hbm, source_hbm, reaction_hbm, pot_ref, vel_ref,
+    counts_ref, turn_ref, source_ref, reaction_ref, load_sem,
     out_face, in_face, face_send, face_recv, mine, sums, sum_send, sum_recv,
     mine_z, sums_z, sum_send_z, sum_recv_z,
 ):
     slab = lax.axis_index("slab")
     cross = lax.axis_index("cross")
+
+    loads = []
+    pairs = ((counts_hbm, counts_ref), (reaction_hbm, reaction_ref), (turn_hbm, turn_ref), (source_hbm, source_ref))
+    for place, (there, here) in enumerate(pairs):
+        loads.append(pltpu.make_async_copy(there, here, load_sem.at[place]))
+        loads[-1].start()
 
     in_face[...] = jnp.zeros_like(in_face)
     barrier = pltpu.get_barrier_semaphore()
@@ -133,6 +140,8 @@
     each(n_cross, greet_cross)
 
     grid = Grid()
+    for each_load in loads:
+        each_load.wait()
     live = counts_ref[slab]
     row8 = iota((8, 128), 0)
     turn = jnp.where(row8 < 2, turn_ref[0], jnp.where(row8 < 4, turn_ref[1], jnp.where(row8 < 6, turn_ref[2], turn_ref[3])))
@@ -311,16 +320,21 @@
     rows, lanes = slots * length, length * length
     dma = pltpu.SemaphoreType.DMA
     vmem = pl.BlockSpec(memory_space=pltpu.VMEM)
-    smem = pl.BlockSpec(memory_space=pltpu.SMEM)
+    hbm = pl.BlockSpec(memory_space=pltpu.HBM)
     potential, velocity = pl.pallas_call(
         functools.partial(kernel, n_slab, n_cross),
         out_shape=(
             jax.ShapeDtypeStruct((rows, lanes), jnp.float32),
             jax.ShapeDtypeStruct((3, rows, lanes), jnp.float32),
         ),
-        in_specs=[smem, smem, vmem, vmem],
+        in_specs=[hbm, hbm, hbm, hbm],
         out_specs=(vmem, vmem),
         scratch_shapes=[
+            pltpu.SMEM(counts.shape, jnp.int32),
+            pltpu.SMEM((slots,), jnp.int32),
+            pltpu.VMEM((rows, lanes), jnp.float32),
+            pltpu.VMEM((rows, lanes), jnp.float32),
+            dma((4,)),
             pltpu.VMEM((2, 4, 8, 128), jnp.float32),
             pltpu.VMEM((2, 4, 8, 128), jnp.float32),
             dma((2, 4)),
@@ -335,7 +349,7 @@
             dma((n_cross,)),
         ],
         compiler_params=pltpu.CompilerParams(
-            collective_id=0, has_side_effects=True, vmem_limit_bytes=16 * 2**20
+            collective_id=0, has_side_effects=True, vmem_limit_bytes=56 * 2**20
         ),
     )(counts, orientation.reshape(slots), source.reshape(rows, lanes), reaction.reshape(rows, lanes))
     return potential.reshape(source.shape), velocity.reshape((3,) + source.shape)

time: 26.8 us -> 27.2 us (1.015)
  Pallas kernels: 22.3 us -> 23.3 us
  local copies, waits for them, and re-layouts: 3.64 us -> 3.09 us
    pallas_call x1, Pallas kernels: 22.3 us -> 23.3 us  [local(): pl.pallas_call(functools.partial(kernel, n_slab, n_cross), out_shape=(jax...]
    unnamed x10 -> x2, local copies, waits for them, and re-layouts: 3.64 us -> 3.09 us
where the time goes in v2:
time: 27.2 us; the launch traced here: 27 us
  Pallas kernels  23.3 us (86%)
  local copies, waits for them, and re-layouts  3.09 us (11%)
  between operations  0.64 us (2%)
    pallas_call x1, Pallas kernels, local(): pl.pallas_call(functools.partial(kernel, n_slab, n_cross), out_shape=(jax...  23.3 us
    unnamed x2, local copies, waits for them, and re-layouts  3.09 us

profile of v2, /device:TPU:0, one launch (start us, length us, event | category | flops | bytes accessed | tf_op | source)
XLA Modules:
  0.0 27.0 jit_solution(3673542397837705555)
XLA Ops:
  0.6 23.3 %shard_map.59 = (f32[64,256]{1,0:T(8,128)}, f32[3,64,256]{2,1,0:T(8,128)}) custom-call(s32[8]{0:T(128)} %counts_hbm.1, s32[4]{0:T(128)} %bitcast.13, f32[64,256]{1,0:T(8,128)} %bitcast.10, f32[64,256]{1,0:T(8,128)} %bitcast.11), custom_call_target="tpu_custom_call" | custom-call | tf_op jit(solution)/shard_map/pallas_call | solution.py:324
  23.9 1.5 %copy.10 = f32[1,4,1,16,256]{4,3,2,1,0:T(8,128)} copy(f32[1,4,1,16,256]{4,3,2,1,0:T(8,128)} %bitcast.12) | data formatting | bytes 131072
  25.4 1.6 %copy.11 = f32[3,1,4,1,16,256]{5,4,3,2,1,0:T(8,128)} copy(f32[3,1,4,1,16,256]{5,4,3,2,1,0:T(8,128)} %bitcast.9) | data formatting | bytes 393216

commit v3 on v2

--- a/solution.py
+++ b/solution.py
@@ -124,7 +124,7 @@
     barrier = pltpu.get_barrier_semaphore()
 
     def each(count, body):
-        if count <= 8:
+        if count <= 32:
             for step in range(1, count):
                 body(step)
         else:
@@ -136,8 +136,21 @@
     def greet_cross(step):
         pl.semaphore_signal(barrier, inc=1, device_id=(slab, lax.rem(cross + step, n_cross)), device_id_type=pl.DeviceIdType.MESH)
 
-    each(n_slab, greet_slab)
-    each(n_cross, greet_cross)
+    devices = n_slab * n_cross
+    direct = devices <= 64
+    me = slab * n_cross + cross
+
+    def seat(k):
+        return k // n_cross, lax.rem(k, n_cross)
+
+    def greet(step):
+        pl.semaphore_signal(barrier, inc=1, device_id=seat(lax.rem(me + step, devices)), device_id_type=pl.DeviceIdType.MESH)
+
+    if direct:
+        each(devices, greet)
+    else:
+        each(n_slab, greet_slab)
+        each(n_cross, greet_cross)
 
     grid = Grid()
     for each_load in loads:
@@ -240,7 +253,7 @@
         return (a * b).reshape(16, 8, 128).sum(0)
 
     z0 = vcycle(grid, r0, inverse, 0)
-    pl.semaphore_wait(barrier, n_slab - 1 + n_cross - 1)
+    pl.semaphore_wait(barrier, devices - 1 if direct else n_slab - 1 + n_cross - 1)
     z_faces = exchange_start(0, z0)
     dot_rz = inner(r0, z0)
     z_rims = exchange_end(0, *z_faces)
@@ -256,7 +269,7 @@
     partial = jnp.concatenate([dot_rz, dot_zq, dot_rw, dot_qw, dot_wv, none, none, none], 0)
     partial = partial.reshape(8, 8, 128).sum(1)
 
-    def total(value, own, count, me, out, into, send, recv, place):
+    def total(value, count, me, out, into, send, recv, place):
         out[...] = value
 
         def copy(source, target):
@@ -280,8 +293,13 @@
         result = into[...].sum(0)
         return result, lambda: each(count, leave)
 
-    across, leave_slab = total(partial, slab, n_slab, slab, mine, sums, sum_send, sum_recv, lambda k: (k, cross))
-    whole, leave_cross = total(across, cross, n_cross, cross, mine_z, sums_z, sum_send_z, sum_recv_z, lambda k: (slab, k))
+    if direct:
+        whole, leave = total(partial, devices, me, mine, sums, sum_send, sum_recv, seat)
+        leaves = (leave,)
+    else:
+        across, leave_slab = total(partial, n_slab, slab, mine, sums, sum_send, sum_recv, lambda k: (k, cross))
+        whole, leave_cross = total(across, n_cross, cross, mine_z, sums_z, sum_send_z, sum_recv_z, lambda k: (slab, k))
+        leaves = (leave_slab, leave_cross)
     whole = jnp.sum(whole, 1, keepdims=True)
     rz, zq, rw, qw, wv = (whole[k : k + 1] for k in range(5))
     alpha = rz / zq
@@ -306,8 +324,8 @@
     store(vel_ref.at[1], keep(alive, 0.5 * (next_v - prev_v + rim_v)))
     store(vel_ref.at[2], keep(alive, 0.5 * (next_w - prev_w)))
 
-    leave_slab()
-    leave_cross()
+    for leave in leaves:
+        leave()
     for turn_of in range(2):
         for side in range(4):
             @pl.when(sides[side][0])
@@ -318,6 +336,7 @@
 def local(n_slab, n_cross, source, reaction, counts, orientation):
     slots, length = source.shape[1], source.shape[3]
     rows, lanes = slots * length, length * length
+    first = n_slab * n_cross if n_slab * n_cross <= 64 else n_slab
     dma = pltpu.SemaphoreType.DMA
     vmem = pl.BlockSpec(memory_space=pltpu.VMEM)
     hbm = pl.BlockSpec(memory_space=pltpu.HBM)
@@ -340,18 +359,23 @@
             dma((2, 4)),
             dma((2, 4)),
             pltpu.VMEM((8, 128), jnp.float32),
-            pltpu.VMEM((n_slab, 8, 128), jnp.float32),
-            dma((n_slab,)),
-            dma((n_slab,)),
+            pltpu.VMEM((first, 8, 128), jnp.float32),
+            dma((first,)),
+            dma((first,)),
             pltpu.VMEM((8, 128), jnp.float32),
             pltpu.VMEM((n_cross, 8, 128), jnp.float32),
             dma((n_cross,)),
             dma((n_cross,)),
         ],
         compiler_params=pltpu.CompilerParams(
-            collective_id=0, has_side_effects=True, vmem_limit_bytes=56 * 2**20
+            collective_id=0, has_side_effects=True, vmem_limit_bytes=16 * 2**20
         ),
-    )(counts, orientation.reshape(slots), source.reshape(rows, lanes), reaction.reshape(rows, lanes))
+    )(
+        *(
+            pltpu.with_memory_space_constraint(x, pltpu.HBM)
+            for x in (counts, orientation.reshape(slots), source.reshape(rows, lanes), reaction.reshape(rows, lanes))
+        )
+    )
     return potential.reshape(source.shape), velocity.reshape((3,) + source.shape)
 
 

time: 27.2 us -> 23.8 us (0.88)
  local copies, waits for them, and re-layouts: 3.09 us -> 1.31 us
  Pallas kernels: 23.3 us -> 21.7 us
    unnamed x2, local copies, waits for them, and re-layouts: 3.09 us -> 1.31 us
    pallas_call x1, Pallas kernels: 23.3 us -> 21.7 us  [local(): pl.pallas_call(functools.partial(kernel, n_slab, n_cross), out_shape=(jax...]
where the time goes in v3:
time: 23.8 us; the launch traced here: 23.6 us
  Pallas kernels  21.7 us (91%)
  local copies, waits for them, and re-layouts  1.31 us (6%)
  between operations  0.64 us (3%)
    pallas_call x1, Pallas kernels, local(): pl.pallas_call(functools.partial(kernel, n_slab, n_cross), out_shape=(jax...  21.7 us
    unnamed x2, local copies, waits for them, and re-layouts  1.31 us

profile of v3, /device:TPU:0, one launch (start us, length us, event | category | flops | bytes accessed | tf_op | source)
XLA Modules:
  0.0 23.6 jit_solution(14704058297146528959)
XLA Ops:
  0.6 21.7 %shard_map.59 = (f32[64,256]{1,0:T(8,128)S(1)}, f32[3,64,256]{2,1,0:T(8,128)S(1)}) custom-call(s32[8]{0:T(128)} %counts_hbm.1, s32[4]{0:T(128)} %bitcast.13, f32[64,256]{1,0:T(8,128)} %bitcast.11, f32[64,256]{1,0:T(8,128)} %bitcast.12), custom_call_target="tpu_custom_call" | custom-call | tf_op jit(solution)/shard_map/pallas_call | solution.py:343
  22.3 0.6 %copy.10 = f32[1,4,1,16,256]{4,3,2,1,0:T(8,128)} copy(f32[1,4,1,16,256]{4,3,2,1,0:T(8,128)S(1)} %bitcast.10) | data formatting | bytes 131072
  23.0 0.7 %copy.11 = f32[3,1,4,1,16,256]{5,4,3,2,1,0:T(8,128)} copy(f32[3,1,4,1,16,256]{5,4,3,2,1,0:T(8,128)S(1)} %bitcast.9) | data formatting | bytes 393216

commit v4 on v3

--- a/solution.py
+++ b/solution.py
@@ -246,8 +246,15 @@
         rim_v = jnp.concatenate([lo, hi], 0)
         return rim_u, rim_v
 
-    def operate(x, rim_u, rim_v):
-        return keep(alive, (6.0 + coef) * x - (grid.near(x, 1) + (rim_u + rim_v)))
+    def interior(x):
+        prev_u, next_u, prev_v, next_v, prev_w, next_w = grid.shifts(x, 1)
+        image = (6.0 + coef) * x - ((prev_u + next_u) + (prev_v + next_v) + (prev_w + next_w))
+        return image, next_u - prev_u, next_v - prev_v, keep(alive, 0.5 * (next_w - prev_w))
+
+    def gradient(inside, rim_u, rim_v):
+        along_u = inside[1] + jnp.where(grid.u == 0, -rim_u, rim_u)
+        along_v = inside[2] + jnp.concatenate([-rim_v[:64], rim_v[64:]], 0)
+        return keep(alive, 0.5 * along_u), keep(alive, 0.5 * along_v), inside[3]
 
     def inner(a, b):
         return (a * b).reshape(16, 8, 128).sum(0)
@@ -256,20 +263,22 @@
     pl.semaphore_wait(barrier, devices - 1 if direct else n_slab - 1 + n_cross - 1)
     z_faces = exchange_start(0, z0)
     dot_rz = inner(r0, z0)
+    z_inside = interior(z0)
     z_rims = exchange_end(0, *z_faces)
-    q0 = operate(z0, *z_rims)
+    q0 = keep(alive, z_inside[0] - (z_rims[0] + z_rims[1]))
     w0 = vcycle(grid, q0, inverse, 0)
     w_faces = exchange_start(1, w0)
     dot_zq = inner(z0, q0)
     dot_rw = inner(r0, w0)
     dot_qw = inner(q0, w0)
+    w_inside = interior(w0)
     w_rims = exchange_end(1, *w_faces)
-    dot_wv = inner(w0, operate(w0, *w_rims))
+    dot_wv = inner(w0, w_inside[0] - (w_rims[0] + w_rims[1]))
     none = jnp.zeros((8, 128), jnp.float32)
     partial = jnp.concatenate([dot_rz, dot_zq, dot_rw, dot_qw, dot_wv, none, none, none], 0)
     partial = partial.reshape(8, 8, 128).sum(1)
 
-    def total(value, count, me, out, into, send, recv, place):
+    def total(value, count, me, out, into, send, recv, place, beside):
         out[...] = value
 
         def copy(source, target):
@@ -288,17 +297,21 @@
             copy(me, lax.rem(me + step, count)).wait_send()
 
         each(count, begin)
+        meanwhile = beside()
         into[me] = value
         each(count, arrive)
         result = into[...].sum(0)
-        return result, lambda: each(count, leave)
+        return result, meanwhile, lambda: each(count, leave)
+
+    def gradients():
+        return gradient(z_inside, *z_rims), gradient(w_inside, *w_rims)
 
     if direct:
-        whole, leave = total(partial, devices, me, mine, sums, sum_send, sum_recv, seat)
+        whole, slopes, leave = total(partial, devices, me, mine, sums, sum_send, sum_recv, seat, gradients)
         leaves = (leave,)
     else:
-        across, leave_slab = total(partial, n_slab, slab, mine, sums, sum_send, sum_recv, lambda k: (k, cross))
-        whole, leave_cross = total(across, n_cross, cross, mine_z, sums_z, sum_send_z, sum_recv_z, lambda k: (slab, k))
+        across, slopes, leave_slab = total(partial, n_slab, slab, mine, sums, sum_send, sum_recv, lambda k: (k, cross), gradients)
+        whole, _, leave_cross = total(across, n_cross, cross, mine_z, sums_z, sum_send_z, sum_recv_z, lambda k: (slab, k), tuple)
         leaves = (leave_slab, leave_cross)
     whole = jnp.sum(whole, 1, keepdims=True)
     rz, zq, rw, qw, wv = (whole[k : k + 1] for k in range(5))
@@ -310,19 +323,13 @@
     of_z = alpha + step * gain
     of_w = -step * alpha
     x = of_z * z0 + of_w * w0
-    rim_u = of_z * z_rims[0] + of_w * w_rims[0]
-    rim_v = of_z * z_rims[1] + of_w * w_rims[1]
-    prev_u, next_u, prev_v, next_v, prev_w, next_w = grid.shifts(x, 1)
-    rim_u = jnp.where(grid.u == 0, -rim_u, rim_u)
-    rim_v = jnp.concatenate([-rim_v[:64], rim_v[64:]], 0)
 
     def store(ref, value):
         ref[...] = jnp.concatenate([value[:64], value[64:]], 1)
 
     store(pot_ref, x)
-    store(vel_ref.at[0], keep(alive, 0.5 * (next_u - prev_u + rim_u)))
-    store(vel_ref.at[1], keep(alive, 0.5 * (next_v - prev_v + rim_v)))
-    store(vel_ref.at[2], keep(alive, 0.5 * (next_w - prev_w)))
+    for part, (of_first, of_second) in enumerate(zip(*slopes)):
+        store(vel_ref.at[part], of_z * of_first + of_w * of_second)
 
     for leave in leaves:
         leave()

time: 23.8 us -> 23.7 us (level)
  no operation moved by 1% of the time
where the time goes in v4:
time: 23.7 us; the launch traced here: 23.6 us
  Pallas kernels  21.6 us (91%)
  local copies, waits for them, and re-layouts  1.31 us (6%)
  between operations  0.64 us (3%)
    pallas_call x1, Pallas kernels, local(): pl.pallas_call(functools.partial(kernel, n_slab, n_cross), out_shape=(jax...  21.6 us
    unnamed x2, local copies, waits for them, and re-layouts  1.31 us

profile of v4, /device:TPU:0, one launch (start us, length us, event | category | flops | bytes accessed | tf_op | source)
XLA Modules:
  0.0 23.6 jit_solution(6528963316302489858)
XLA Ops:
  0.6 21.6 %shard_map.59 = (f32[64,256]{1,0:T(8,128)S(1)}, f32[3,64,256]{2,1,0:T(8,128)S(1)}) custom-call(s32[8]{0:T(128)} %counts_hbm.1, s32[4]{0:T(128)} %bitcast.13, f32[64,256]{1,0:T(8,128)} %bitcast.11, f32[64,256]{1,0:T(8,128)} %bitcast.12), custom_call_target="tpu_custom_call" | custom-call | tf_op jit(solution)/shard_map/pallas_call | solution.py:350
  22.2 0.6 %copy.10 = f32[1,4,1,16,256]{4,3,2,1,0:T(8,128)} copy(f32[1,4,1,16,256]{4,3,2,1,0:T(8,128)S(1)} %bitcast.10) | data formatting | bytes 131072
  22.9 0.7 %copy.11 = f32[3,1,4,1,16,256]{5,4,3,2,1,0:T(8,128)} copy(f32[3,1,4,1,16,256]{5,4,3,2,1,0:T(8,128)S(1)} %bitcast.9) | data formatting | bytes 393216

commit v5 on v4

--- a/solution.py
+++ b/solution.py
@@ -276,7 +276,8 @@
     dot_wv = inner(w0, w_inside[0] - (w_rims[0] + w_rims[1]))
     none = jnp.zeros((8, 128), jnp.float32)
     partial = jnp.concatenate([dot_rz, dot_zq, dot_rw, dot_qw, dot_wv, none, none, none], 0)
-    partial = partial.reshape(8, 8, 128).sum(1)
+    partial = jnp.sum(partial.reshape(8, 8, 128).sum(1), 1, keepdims=True)
+    partial = jnp.sum(keep(iota((8, 128), 1) == row8, partial), 0, keepdims=True)
 
     def total(value, count, me, out, into, send, recv, place, beside):
         out[...] = value
@@ -313,8 +314,7 @@
         across, slopes, leave_slab = total(partial, n_slab, slab, mine, sums, sum_send, sum_recv, lambda k: (k, cross), gradients)
         whole, _, leave_cross = total(across, n_cross, cross, mine_z, sums_z, sum_send_z, sum_recv_z, lambda k: (slab, k), tuple)
         leaves = (leave_slab, leave_cross)
-    whole = jnp.sum(whole, 1, keepdims=True)
-    rz, zq, rw, qw, wv = (whole[k : k + 1] for k in range(5))
+    rz, zq, rw, qw, wv = (whole[:, k : k + 1] for k in range(5))
     alpha = rz / zq
     rz_new = rz - alpha * (zq + rw) + alpha * alpha * qw
     gain = 1.0 + rz_new / rz
@@ -365,12 +365,12 @@
             pltpu.VMEM((2, 4, 8, 128), jnp.float32),
             dma((2, 4)),
             dma((2, 4)),
-            pltpu.VMEM((8, 128), jnp.float32),
-            pltpu.VMEM((first, 8, 128), jnp.float32),
+            pltpu.VMEM((1, 128), jnp.float32),
+            pltpu.VMEM((first, 1, 128), jnp.float32),
             dma((first,)),
             dma((first,)),
-            pltpu.VMEM((8, 128), jnp.float32),
-            pltpu.VMEM((n_cross, 8, 128), jnp.float32),
+            pltpu.VMEM((1, 128), jnp.float32),
+            pltpu.VMEM((n_cross, 1, 128), jnp.float32),
             dma((n_cross,)),
             dma((n_cross,)),
         ],

time: 23.7 us -> 23 us (0.970)
  Pallas kernels: 21.6 us -> 20.9 us
    pallas_call x1, Pallas kernels: 21.6 us -> 20.9 us  [local(): pl.pallas_call(functools.partial(kernel, n_slab, n_cross), out_shape=(jax...]
where the time goes in v5:
time: 23 us; the launch traced here: 22.9 us
  Pallas kernels  20.9 us (91%)
  local copies, waits for them, and re-layouts  1.31 us (6%)
  between operations  0.64 us (3%)
    pallas_call x1, Pallas kernels, local(): pl.pallas_call(functools.partial(kernel, n_slab, n_cross), out_shape=(jax...  20.9 us
    unnamed x2, local copies, waits for them, and re-layouts  1.31 us

profile of v5, /device:TPU:0, one launch (start us, length us, event | category | flops | bytes accessed | tf_op | source)
XLA Modules:
  0.0 22.9 jit_solution(7218496447565149673)
XLA Ops:
  0.6 20.9 %shard_map.59 = (f32[64,256]{1,0:T(8,128)S(1)}, f32[3,64,256]{2,1,0:T(8,128)S(1)}) custom-call(s32[8]{0:T(128)} %counts_hbm.1, s32[4]{0:T(128)} %bitcast.13, f32[64,256]{1,0:T(8,128)} %bitcast.11, f32[64,256]{1,0:T(8,128)} %bitcast.12), custom_call_target="tpu_custom_call" | custom-call | tf_op jit(solution)/shard_map/pallas_call | solution.py:350
  21.6 0.6 %copy.10 = f32[1,4,1,16,256]{4,3,2,1,0:T(8,128)} copy(f32[1,4,1,16,256]{4,3,2,1,0:T(8,128)S(1)} %bitcast.10) | data formatting | bytes 131072
  22.2 0.7 %copy.11 = f32[3,1,4,1,16,256]{5,4,3,2,1,0:T(8,128)} copy(f32[3,1,4,1,16,256]{5,4,3,2,1,0:T(8,128)S(1)} %bitcast.9) | data formatting | bytes 393216
